TPU v7x, 128 devices: a whole 4x4x4 slice. The times are simulated.
128 devices in a mesh: dp: 4 (over x), ctx: 32 (over z, y, core).
Axes of the slice: x: 4, y: 4, z: 4, core: 2. Of those that a mesh axis runs over, the one named last changes fastest.
Arguments:
- queries: bfloat16 [4, 4096, 2048], P('dp', 'ctx'), may hold values from -21 to 21
- key_rows: bfloat16 [4, 4096, 512], P('dp', 'ctx'), may hold values from -21 to 21
- value_row_blocks: bfloat16 [4, 4096, 512], P('dp', 'ctx'), may hold values from -6 to 6
- out_grad: bfloat16 [4, 4096, 2048], P('dp', 'ctx'), may hold values from -6 to 6
- segment_ids: int32 [4, 4096], P('dp', 'ctx'), may hold values from 0 to 15, never falling along the last dimension, each value on 1 to 2304 neighbouring positions
- block_plan: int32 [4, 32], P('dp', 'ctx'), may hold values from 0 to 3, as said below
Outputs:
- attended: bfloat16 [4, 4096, 2048], P('dp', 'ctx')
- query_grad: bfloat16 [4, 4096, 2048], P('dp', 'ctx')
- key_grad: bfloat16 [4, 4096, 512], P('dp', 'ctx')
- value_grad: bfloat16 [4, 4096, 512], P('dp', 'ctx')
Inputs may be any that keep to these rules, and one draw needn't show every extreme that they name: For every block b, block_plan[d, b] over the 4 values of d names every sequence once.
All inputs are finite; a program needn't handle non-finite values.
Results may differ from a plain program's by a relative error of at most 0.025.
Values may be sent and summed in bfloat16 or wider, within the bound.
A program may use at most 128 MiB of HBM per device.

v0:
```python
import math

import jax
import jax.numpy as jnp
from jax import lax
from jax.sharding import PartitionSpec as P

QUERY_HEADS = 16
KEY_VALUE_HEADS = 4
HEAD_SIZE = 128


def select_rows(gathered, chosen):
    sources, row_total, feature = gathered.shape
    blocks = chosen.shape[1]
    shaped = gathered.reshape(sources, blocks, row_total // blocks, feature)
    selected = jnp.where(chosen[:, :, None, None], shaped, jnp.zeros((), gathered.dtype))
    return jnp.sum(selected, axis=0).reshape(row_total, feature)


def body(queries, key_rows, value_row_blocks, out_grad, segment_ids, block_plan):
    attn_scale = 1.0 / math.sqrt(HEAD_SIZE)
    query_group_width = QUERY_HEADS // KEY_VALUE_HEADS
    key_value_width = KEY_VALUE_HEADS * HEAD_SIZE
    dp_size = lax.axis_size("dp")
    ctx_size = lax.axis_size("ctx")
    my_seq = lax.axis_index("dp")
    my_shard = lax.axis_index("ctx")
    resident_rows = queries.shape[1]
    packed_length = resident_rows * ctx_size
    grouped_query, g_key, g_value, grouped_gradient, g_plan = (
        lax.all_gather(queries, "dp", axis=0, tiled=True),
        lax.all_gather(key_rows, "dp", axis=0, tiled=True),
        lax.all_gather(value_row_blocks, "dp", axis=0, tiled=True),
        lax.all_gather(out_grad, "dp", axis=0, tiled=True),
        lax.all_gather(block_plan, "dp", axis=0, tiled=True),
    )
    incoming_blocks = g_plan == my_seq
    query_resident = select_rows(grouped_query, incoming_blocks).reshape(
        resident_rows, KEY_VALUE_HEADS, query_group_width, HEAD_SIZE
    )
    gradient_resident = select_rows(grouped_gradient, incoming_blocks).reshape(
        resident_rows, KEY_VALUE_HEADS, query_group_width, HEAD_SIZE
    )
    kv_local = jnp.concatenate(
        [select_rows(g_key, incoming_blocks), select_rows(g_value, incoming_blocks)], axis=1
    )
    own_segs = segment_ids[0]
    gathered_key_value, all_segs = (
        lax.all_gather(kv_local, "ctx", axis=0, tiled=True),
        lax.all_gather(own_segs, "ctx", axis=0, tiled=True),
    )
    key_block = min(512, packed_length)
    key_gathered = gathered_key_value[:, :key_value_width].reshape(
        packed_length, KEY_VALUE_HEADS, HEAD_SIZE
    )
    value_gathered = gathered_key_value[:, key_value_width:].reshape(
        packed_length, KEY_VALUE_HEADS, HEAD_SIZE
    )
    query_pos = my_shard * resident_rows + jnp.arange(resident_rows, dtype=jnp.int32)
    block_total = packed_length // key_block
    block_ids = jnp.arange(block_total, dtype=jnp.int32)

    def masked_scores(first_key, key_count):
        keys_part = lax.dynamic_slice_in_dim(key_gathered, first_key, key_count, 0)
        values_part = lax.dynamic_slice_in_dim(value_gathered, first_key, key_count, 0)
        segs_part = lax.dynamic_slice_in_dim(all_segs, first_key, key_count, 0)
        key_pos = first_key + jnp.arange(key_count, dtype=jnp.int32)
        visible = (
            (segs_part[None, :] == own_segs[:, None])
            & (key_pos[None, :] <= query_pos[:, None])
            & (key_pos[None, :] >= 0)
        )
        scores = (
            jnp.einsum(
                "tkgd,skd->kgts", query_resident, keys_part, preferred_element_type=jnp.float32
            )
            * attn_scale
        )
        return (jnp.where(visible[None, None], scores, -jnp.inf), keys_part, values_part)

    def stat_step(carried, block_index):
        first_key = block_index * key_block
        running, totals = carried
        masked, _, _ = masked_scores(first_key, key_block)
        newtop = jnp.maximum(running, jnp.max(masked, axis=-1))
        totals = totals * jnp.exp(running - newtop) + jnp.sum(
            jnp.exp(masked - newtop[..., None]), axis=-1
        )
        return ((newtop, totals), None)

    statistic_shape = (KEY_VALUE_HEADS, query_group_width, resident_rows)
    stat_init = (
        jnp.full(statistic_shape, -1e30, jnp.float32),
        jnp.zeros(statistic_shape, jnp.float32),
    )
    (running, totals), _ = lax.scan(stat_step, stat_init, block_ids)
    log_total = running + jnp.log(totals)

    def out_step(carried, block_index):
        first_key = block_index * key_block
        masked, _, values_part = masked_scores(first_key, key_block)
        weight_half = jnp.exp(masked - log_total[..., None]).astype(jnp.bfloat16)
        return (
            carried
            + jnp.einsum(
                "kgts,skd->tkgd", weight_half, values_part, preferred_element_type=jnp.float32
            ),
            None,
        )

    zero_rows = jnp.zeros(
        (resident_rows, KEY_VALUE_HEADS, query_group_width, HEAD_SIZE), jnp.float32
    )
    out_acc, _ = lax.scan(out_step, zero_rows, block_ids)
    attended_local = out_acc.astype(jnp.bfloat16)
    row_delta = jnp.sum(
        gradient_resident.astype(jnp.float32) * attended_local.astype(jnp.float32), axis=-1
    ).transpose(1, 2, 0)

    def grad_pieces(first_key, key_count):
        masked, keys_part, values_part = masked_scores(first_key, key_count)
        weights = jnp.exp(masked - log_total[..., None])
        weight_half = weights.astype(jnp.bfloat16)
        weight_grad = jnp.einsum(
            "tkgd,skd->kgts", gradient_resident, values_part, preferred_element_type=jnp.float32
        )
        score_grad = (weights * (weight_grad - row_delta[..., None]) * attn_scale).astype(
            jnp.bfloat16
        )
        return (score_grad, weight_half, keys_part)

    def key_terms(score_grad, weight_half, key_count):
        key_term = jnp.einsum(
            "kgts,tkgd->skd", score_grad, query_resident, preferred_element_type=jnp.float32
        )
        value_term = jnp.einsum(
            "kgts,tkgd->skd", weight_half, gradient_resident, preferred_element_type=jnp.float32
        )
        return jnp.concatenate(
            [
                key_term.reshape(key_count, key_value_width),
                value_term.reshape(key_count, key_value_width),
            ],
            axis=1,
        )

    def grad_step(carried, block_index):
        first_key = block_index * key_block
        score_grad, weight_half, keys_part = grad_pieces(first_key, key_block)
        query_term = jnp.einsum(
            "kgts,skd->tkgd", score_grad, keys_part, preferred_element_type=jnp.float32
        )
        return (carried + query_term, key_terms(score_grad, weight_half, key_block))

    query_acc, stacked = lax.scan(grad_step, zero_rows, block_ids)
    key_grads = lax.psum_scatter(
        stacked.reshape(packed_length, 2 * key_value_width), "ctx", scatter_dimension=0, tiled=True
    )
    query_half = query_acc.astype(jnp.bfloat16).reshape(resident_rows, QUERY_HEADS * HEAD_SIZE)
    key_half = key_grads.astype(jnp.bfloat16)
    attended_flat = attended_local.reshape(resident_rows, QUERY_HEADS * HEAD_SIZE)
    back_out, back_query, back_kv = (
        lax.all_gather(attended_flat[None], "dp", axis=0, tiled=True),
        lax.all_gather(query_half[None], "dp", axis=0, tiled=True),
        lax.all_gather(key_half[None], "dp", axis=0, tiled=True),
    )
    outgoing = jnp.arange(dp_size, dtype=jnp.int32)[:, None] == block_plan[0][None, :]
    attended = select_rows(back_out, outgoing)[None]
    query_grad = select_rows(back_query, outgoing)[None]
    kv_plan = select_rows(back_kv, outgoing)
    return (
        attended,
        query_grad,
        kv_plan[:, :key_value_width][None],
        kv_plan[:, key_value_width:][None],
    )


def solution(mesh):
    in_specs = (
        P("dp", "ctx", None),
        P("dp", "ctx", None),
        P("dp", "ctx", None),
        P("dp", "ctx", None),
        P("dp", "ctx"),
        P("dp", "ctx"),
    )
    out_specs = (
        P("dp", "ctx", None),
        P("dp", "ctx", None),
        P("dp", "ctx", None),
        P("dp", "ctx", None),
    )
    return jax.shard_map(body, mesh=mesh, in_specs=in_specs, out_specs=out_specs, check_vma=False)
```

profile of v0, /device:TPU:1, one launch (start us, length us, event | category | flops | bytes accessed | tf_op | source)
XLA Modules:
  0.0 613.1 jit_solution(5799216000926603723)
XLA Ops:
  11.3 7.7 %all-reduce = s32[4]{0:T(128)S(1)} all-reduce(s32[4]{0:T(128)S(1)} %bitcast_dynamic-update-slice_fusion), channel_id=1, replica_groups=mesh['dp'=4,'ctx'=32] {'dp'}, use_global_device_ids=true, to_apply=%add | all-reduce | flops 4 | bytes 32
  19.0 13.3 %all_gather.31 = bf16[4,128,512]{2,1,0:T(8,128)(2,1)S(1)} all-gather(bf16[1,128,512]{2,1,0:T(8,128)(2,1)} %param.13), channel_id=1, replica_groups=mesh['dp'=4,'ctx'=32] {'dp'}, dimensions={0}, use_global_device_ids=true | all-gather | bytes 655360 | tf_op jit(solution)/shard_map/all_gather | solution.py:33
  32.3 13.5 %all_gather.32 = bf16[4,128,512]{2,1,0:T(8,128)(2,1)S(1)} all-gather(bf16[1,128,512]{2,1,0:T(8,128)(2,1)} %param.14), channel_id=1, replica_groups=mesh['dp'=4,'ctx'=32] {'dp'}, dimensions={0}, use_global_device_ids=true | all-gather | bytes 655360 | tf_op jit(solution)/shard_map/all_gather | solution.py:34
  46.9 28.7 %all-gather = s32[1,4096]{1,0:T(1,128)S(1)} all-gather(s32[1,128]{1,0:T(1,128)S(1)} %copy-done.5), channel_id=2, replica_groups=mesh['dp'=4,'ctx'=32] {'ctx'}, dimensions={1}, use_global_device_ids=true | all-gather | bytes 16896 | tf_op jit(solution)/shard_map/all_gather | solution.py:51
  75.6 7.6 %all-gather.11.cloned.1.call-done = bf16[4,128,2048]{2,1,0:T(8,128)(2,1)} async-done(((bf16[1,128,2048]{2,1,0:T(8,128)(2,1)}), bf16[4,128,2048]{2,1,0:T(8,128)(2,1)}) %all-gather.11.cloned.1.call-update) | async-done | bytes 2097168 | tf_op jit(solution)/shard_map/all_gather | solution.py:32
  83.2 3.6 select_reduce_fusion.1
  88.1 51.5 %all-gather.9.cloned.1.call-done = bf16[4096,1024]{1,0:T(8,128)(2,1)} async-done(((bf16[128,1024]{1,0:T(8,128)(2,1)}), bf16[4096,1024]{1,0:T(8,128)(2,1)}) %all-gather.9.cloned.1.call-update) | async-done | bytes 8388624 | tf_op jit(solution)/shard_map/all_gather | solution.py:50
  139.6 5.7 fusion.53
  145.3 6.4 %copy.45 = bf16[4096,512]{0,1:T(8,128)(2,1)} copy(bf16[4096,512]{1,0:T(8,128)(2,1)} %get-tuple-element.449) | data formatting | bytes 8388608 | tf_op jit(solution)/shard_map/slice | solution.py:54
  151.7 6.3 %copy.48 = bf16[4096,4,128]{2,0,1:T(8,128)(2,1)} copy(bf16[4096,4,128]{0,2,1:T(8,128)(2,1)} %bitcast.198) | data formatting | bytes 8388608
  158.0 67.8 %while.37 = (s32[]{:T(128)}, f32[4,4,128]{2,1,0:T(4,128)S(1)}, f32[4,4,128]{2,1,0:T(4,128)S(1)}, s32[8]{0:T(128)S(1)}, s32[4096]{0:T(1024)S(1)}, /*index=5*/s32[...) while((s32[]{:T(128)}, f32[4,4,128]{2,1,0:T(4,128)S(1)}, ...), condition=%wide.region_6.7_spmd.clone, body=%wide.region_3.0_spmd.clone.sunk | while | flops 276049536 | bytes 9753310 | solution.py:97
  159.6 3.7 fusion.86
  163.4 3.1 exponential_reduce_fusion.2
  168.1 3.7 fusion.86
  171.8 3.1 exponential_reduce_fusion.2
  176.6 3.7 fusion.86
  180.3 3.1 exponential_reduce_fusion.2
  185.1 3.7 fusion.86
  188.8 3.1 exponential_reduce_fusion.2
  193.5 3.7 fusion.86
  197.3 3.1 exponential_reduce_fusion.2
  202.0 3.7 fusion.86
  205.7 3.1 exponential_reduce_fusion.2
  210.5 3.7 fusion.86
  214.2 3.1 exponential_reduce_fusion.2
  219.0 3.7 fusion.86
  222.7 3.1 exponential_reduce_fusion.2
  225.8 6.5 %copy.44 = bf16[4096,512]{0,1:T(8,128)(2,1)} copy(bf16[4096,512]{1,0:T(8,128)(2,1)} %get-tuple-element.448) | data formatting | bytes 8388608 | tf_op jit(solution)/shard_map/slice | solution.py:57
  232.3 35.2 %while.38 = (s32[]{:T(128)}, f32[128,4,4,128]{0,3,2,1:T(8,128)S(1)}, s32[8]{0:T(128)S(1)}, bf16[4096,4,128]{0,2,1:T(8,128)(2,1)}, s32[4096]{0:T(1024)S(1)}, /*in...) while((s32[]{:T(128)}, ...), condition=%wide.region_8.9_spmd.clone, body=%wide.region_7.8_spmd.clone.sunk | while | flops 541853312 | bytes 3823840 | solution.py:115
  268.5 130.9 %while.39 = (s32[]{:T(128)}, f32[128,4,4,128]{0,3,2,1:T(8,128)}, f32[8,512,1024]{2,1,0:T(8,128)}, s32[8]{0:T(128)S(1)}, bf16[4096,4,128]{2,0,1:T(8,128)(2,1)}, /...) while((s32[]{:T(128)}, f32[128,4,4,128]{0,3,2,1:T(8,128)}, ...), condition=%wide.region_13.14_spmd.clone, body=%wide.region_12.13_spmd.clone.sunk | while | flops 1355024000 | bytes 73110336 | solution.py:156
  271.9 3.1 fusion.103
  288.0 3.1 fusion.103
  291.1 3.0 fusion.104
  304.3 3.1 fusion.103
  307.4 3.0 fusion.104
  320.7 3.1 fusion.103
  323.8 3.0 fusion.104
  337.2 3.1 fusion.103
  353.6 3.1 fusion.103
  370.0 3.1 fusion.103
  373.1 3.0 fusion.104
  386.4 3.1 fusion.103
  389.5 3.0 fusion.104
  402.9 109.9 %reduce-scatter.2.cloned.1.call-done = f32[128,1024]{1,0:T(8,128)} async-done(((f32[4096,1024]{1,0:T(8,128)}), f32[128,1024]{1,0:T(8,128)}) %reduce-scatter.2.cloned.1.call-update) | async-done | bytes 524304 | tf_op jit(solution)/shard_map/reduce_scatter | solution.py:157
  514.7 31.5 %all-gather.17.cloned.1.call-done = bf16[4,128,2048]{2,1,0:T(8,128)(2,1)} async-done(((bf16[1,128,2048]{2,1,0:T(8,128)(2,1)}), bf16[4,128,2048]{2,1,0:T(8,128)(2,1)}) %all-gather.17.cloned.1.call-update) | async-done | bytes 2097168 | tf_op jit(solution)/shard_map/all_gather | solution.py:165
  546.3 33.0 %all-gather.13.cloned.1.call-done = bf16[4,128,2048]{2,1,0:T(8,128)(2,1)} async-done(((bf16[1,128,2048]{2,1,0:T(8,128)(2,1)}), bf16[4,128,2048]{2,1,0:T(8,128)(2,1)}) %all-gather.13.cloned.1.call-update) | async-done | bytes 2097168 | tf_op jit(solution)/shard_map/all_gather | solution.py:164
  579.2 4.5 select_reduce_fusion
  583.7 20.2 %all-gather.19.cloned.1.call-done = bf16[512,1024]{1,0:T(8,128)(2,1)} async-done(((bf16[128,1024]{1,0:T(8,128)(2,1)}), bf16[512,1024]{1,0:T(8,128)(2,1)}) %all-gather.19.cloned.1.call-update) | async-done | bytes 1048592 | tf_op jit(solution)/shard_map/all_gather | solution.py:166
  (309 shorter events, 137.0 us)
Async XLA Ops:
  7.2 39.7 %copy-start.5 = (s32[1,128]{1,0:T(1,128)S(1)}, s32[1,128]{1,0:T(1,128)}, u32[]{:S(2)}) copy-start(s32[1,128]{1,0:T(1,128)} %param.16) | copy-start | bytes 1540
  7.2 68.5 %all-gather.15.cloned.1.call-start = ((), (), s32[]{:S(2)}) async-start(), calls=%async_computation.4 | async-start | bytes 2621440 | tf_op jit(solution)/shard_map/all_gather | solution.py:35
  7.9 75.3 %all-gather.11.cloned.1.call-start = ((), (), s32[]{:S(2)}) async-start(), calls=%async_computation.2 | async-start | bytes 2621440 | tf_op jit(solution)/shard_map/all_gather | solution.py:32
  8.7 130.9 %all-gather.9.cloned.1.call-start = ((), (), s32[]{:S(2)}) async-start(), calls=%async_computation.1 | async-start | bytes 8650752 | tf_op jit(solution)/shard_map/all_gather | solution.py:50
  46.8 466.1 %reduce-scatter.2.cloned.1.call-start = ((), (), s32[]{:S(2)}) async-start(), calls=%async_computation.6 | async-start | bytes 17301504 | tf_op jit(solution)/shard_map/reduce_scatter | solution.py:157
  225.8 6.5 %copy-start.4 = (f32[128,4,4,128]{0,3,2,1:T(8,128)S(1)}, f32[128,4,4,128]{0,3,2,1:T(8,128)}, u32[]{:S(2)}) copy-start(f32[128,4,4,128]{0,3,2,1:T(8,128)} %custom-call.2) | copy-start | bytes 3145732
  271.5 3.5 copy-start
  275.0 2.7 copy-start.1
  287.6 3.5 copy-start
  291.0 3.0 copy-start.1
  304.0 3.5 copy-start
  307.4 3.0 copy-start.1
  320.4 3.5 copy-start
  323.8 3.0 copy-start.1
  336.8 3.5 copy-start
  340.2 3.0 copy-start.1
  353.2 3.5 copy-start
  356.7 3.0 copy-start.1
  369.6 3.5 copy-start
  373.1 3.0 copy-start.1
  386.0 3.5 copy-start
  389.5 3.0 copy-start.1
  399.5 1.2 copy-start.2
  399.5 2.4 copy-start.3
  399.5 146.8 %all-gather.17.cloned.1.call-start = ((), (), s32[]{:S(2)}) async-start(), calls=%async_computation.5 | async-start | bytes 2621440 | tf_op jit(solution)/shard_map/all_gather | solution.py:165
  401.8 177.4 %all-gather.13.cloned.1.call-start = ((), (), s32[]{:S(2)}) async-start(), calls=%async_computation.3 | async-start | bytes 2621440 | tf_op jit(solution)/shard_map/all_gather | solution.py:164
  402.9 201.1 %all-gather.19.cloned.1.call-start = ((), (), s32[]{:S(2)}) async-start(), calls=%async_computation.7 | async-start | bytes 1310720 | tf_op jit(solution)/shard_map/all_gather | solution.py:166
Sparse Core Ops, SparseCore 0:
  9.7 40.9 all-gather.14
  52.3 30.8 all-gather.10
  86.1 53.4 all-gather.8
  399.6 113.2 reduce-scatter.1
  515.0 31.2 all-gather.16
  548.3 30.8 all-gather.12
  580.9 23.0 all-gather.18
where the time goes:
time: 616 us; the launch traced here: 613 us
  waiting for transfers between devices  255 us (41%)
  matrix products  130 us (21%)
  local copies, waits for them, and re-layouts  75.2 us (12%)
  blocking collectives  63.2 us (10%)
  other arithmetic  57.4 us (9%)
  loops' own time  17.3 us (3%)
  between operations  14.9 us (2%)
    reduce_scatter x1, waiting for transfers between devices, body(): lax.psum_scatter(stacked.reshape(packed_length, 2 * key_value_width), 'ct...  110 us
    all_gather x1, waiting for transfers between devices, body(): lax.all_gather(kv_local, 'ctx', axis=0, tiled=True)  51.5 us
    dot_general x16, matrix products, masked_scores(): jnp.einsum('tkgd,skd->kgts', query_resident, keys_part, preferred_element...  43.7 us
    all_gather x1, waiting for transfers between devices, body(): lax.all_gather(attended_flat[None], 'dp', axis=0, tiled=True)  33 us
    all_gather x1, waiting for transfers between devices, body(): lax.all_gather(query_half[None], 'dp', axis=0, tiled=True)  31.5 us
    all_gather x1, blocking collectives, body(): lax.all_gather(own_segs, 'ctx', axis=0, tiled=True)  28.7 us
    dynamic_update_slice x16, local copies, waits for them, and re-layouts, body(): query_acc, stacked = lax.scan(grad_step, zero_rows, block_ids)  27.1 us
    reduce_sum x8, other arithmetic, stat_step(): jnp.sum(jnp.exp(masked - newtop[..., None]), axis=-1)  24.5 us
  transfers between devices with their start and end apart: 7, of which 6 were waited for; matrix products, arithmetic and copies ran while one was open for 3% of the time, Pallas kernels for 0%

commit v1 on v0

v1 whole, which is shorter than its diff:
```python
import math

import jax
import jax.numpy as jnp
from jax import lax
from jax.experimental import pallas as pl
from jax.experimental.pallas import tpu as pltpu
from jax.sharding import PartitionSpec as P

MESH = pl.DeviceIdType.MESH
BF16 = jnp.bfloat16
F32 = jnp.float32

BLK = 128
HEAD = 128
GROUP = 4
GW = GROUP * HEAD
SIDE = 4
RING = 8
NBLK = 32
DOCS = 16
OFFSETS = (1, 3, 2)
CHUNK = 256
MOST = 10
PARTS = 2
PART = BLK // PARTS
NEG = -1e30


def place():
    x = lax.axis_index("dp")
    c = lax.axis_index("ctx")
    return x, lax.div(c, 8), lax.rem(lax.div(c, 2), 4), lax.rem(c, 2)


def remote(src, dst, send, recv, device):
    return pltpu.make_async_remote_copy(
        src_ref=src, dst_ref=dst, send_sem=send, recv_sem=recv, device_id=device, device_id_type=MESH
    )


def ahead(i, o):
    return lax.rem(i + o, 4)


def behind(i, o):
    return lax.rem(i + 4 - o, 4)


def ctx_of(z, y, core):
    return z * 8 + y * 2 + core


def lanes(i, width):
    return pl.ds(pl.multiple_of(i * width, width), width)


def one_hot(values, wanted):
    return jnp.where(values == wanted, 1.0, 0.0).astype(BF16)


def pick(weights, parts):
    width = parts[0].shape[1]
    tiles = []
    for t in range(width // 128):
        total = None
        for w, part in zip(weights, parts):
            term = part[:, t * 128 : (t + 1) * 128] * w
            total = term if total is None else total + term
        tiles.append(total)
    return tiles


def put(ref, tiles, base=None):
    for t, tile in enumerate(tiles):
        if base is None:
            ref[:, t * 128 : (t + 1) * 128] = tile
        else:
            ref[:, pl.ds(pl.multiple_of(base + t * 128, 128), 128)] = tile


def enter(devices):
    barrier = pltpu.get_barrier_semaphore()
    for device in devices:
        pl.semaphore_signal(barrier, inc=1, device_id=device, device_id_type=MESH)
    pl.semaphore_wait(barrier, len(devices))


def gather_kernel(
    q, k, v, g, seg, plan,
    qb, gb, kv, segs, planes,
    meta, a_kv, a_q, a_g, s_kv, s_q, s_g,
    xs, xr, zs, zr, ys, yr, cs, cr, fs, fr, ms, mr,
):
    x, z, y, core = place()
    ring = y * 2 + core
    x_dev = [(ahead(x, o), ctx_of(z, y, core)) for o in OFFSETS]
    z_dev = [(x, ctx_of(ahead(z, o), y, core)) for o in OFFSETS]
    y_dev = [(x, ctx_of(z, ahead(y, o), core)) for o in OFFSETS]
    w_dev = [(x, ctx_of(z, ahead(y, o), 1 - core)) for o in OFFSETS]
    c_dev = (x, ctx_of(z, y, 1 - core))

    meta[...] = jnp.broadcast_to(plan[...], (8, 128))
    meta[0:1, :] = seg[...]
    enter(x_dev + z_dev + y_dev + w_dev + [c_dev])

    x_cps = []
    for item in range(3 + 2 * PARTS):
        row = []
        for i, o in enumerate(OFFSETS):
            t = ahead(x, o)
            if item == 0:
                src, dst = meta, planes.at[x]
            elif item == 1:
                src, dst = k.at[:, lanes(t, HEAD)], a_kv.at[x, :, pl.ds(0, HEAD)]
            elif item == 2:
                src, dst = v.at[:, lanes(t, HEAD)], a_kv.at[x, :, pl.ds(HEAD, HEAD)]
            else:
                whole, land = ((q, a_q), (g, a_g))[(item - 3) // PARTS]
                rows = pl.ds(((item - 3) % PARTS) * PART, PART)
                src, dst = whole.at[rows, lanes(t, GW)], land.at[x, rows]
            cp = remote(src, dst, xs.at[i, item], xr.at[i, item], x_dev[i])
            cp.start()
            row.append(cp)
        x_cps.append(row)
    planes[x] = meta[...]
    a_kv[x, :, 0:HEAD] = k[:, lanes(x, HEAD)]
    a_kv[x, :, HEAD : 2 * HEAD] = v[:, lanes(x, HEAD)]
    a_q[x] = q[:, lanes(x, GW)]
    a_g[x] = g[:, lanes(x, GW)]

    def arrived(item):
        for cp in x_cps[item]:
            cp.wait_recv()

    arrived(0)
    m_z = []
    for i, o in enumerate(OFFSETS):
        cp = remote(planes.at[ahead(z, o)], segs.at[z, ring], zs.at[i, 0], zr.at[i, 0], z_dev[i])
        cp.start()
        m_z.append(cp)
    segs[z, ring] = planes[z]
    held = [planes[d, 1:2, :] for d in range(SIDE)]
    hots = [[one_hot(h, ahead(z, o)) for h in held] for o in OFFSETS]
    own_hot = [one_hot(h, z) for h in held]

    arrived(1)
    arrived(2)
    kv_z = []
    parts = [a_kv[d] for d in range(SIDE)]
    for i, o in enumerate(OFFSETS):
        put(s_kv.at[i], pick(hots[i], parts))
        cp = remote(s_kv.at[i], kv.at[z, ring], zs.at[i, 1], zr.at[i, 1], z_dev[i])
        cp.start()
        kv_z.append(cp)
    put(kv.at[z, ring], pick(own_hot, parts))

    y_cps, c_cps, f_cps = [], [], []

    def spread(p):
        zp = z if p == 0 else behind(z, OFFSETS[p - 1])
        row = []
        for i in range(3):
            cp = remote(kv.at[zp, ring], kv.at[zp, ring], ys.at[p, i], yr.at[p, i], y_dev[i])
            cp.start()
            row.append(cp)
        y_cps.append(row)
        cp = remote(kv.at[zp, ring], kv.at[zp, ring], cs.at[p], cr.at[p], c_dev)
        cp.start()
        c_cps.append(cp)

    def pass_on(p):
        zp = z if p == 0 else behind(z, OFFSETS[p - 1])
        for i, o in enumerate(OFFSETS):
            there = behind(y, o) * 2 + core
            y_cps[p][i].wait_recv()
            cp = remote(kv.at[zp, there], kv.at[zp, there], fs.at[p, i], fr.at[p, i], c_dev)
            cp.start()
            f_cps.append(cp)

    big_z = []

    def rows_over_z(item):
        which, part = (item - 3) // PARTS, (item - 3) % PARTS
        land, stage, out = ((a_q, s_q, qb), (a_g, s_g, gb))[which]
        rows = pl.ds(part * PART, PART)
        arrived(item)
        got = [land[d, part * PART : (part + 1) * PART] for d in range(SIDE)]
        for i, o in enumerate(OFFSETS):
            put(stage.at[i, rows], pick(hots[i], got))
            cp = remote(stage.at[i, rows], out.at[z, rows], zs.at[i, item - 1], zr.at[i, item - 1], z_dev[i])
            cp.start()
            big_z.append(cp)
        put(out.at[z, rows], pick(own_hot, got))

    spread(0)
    for p in range(3):
        kv_z[p].wait_recv()
        spread(p + 1)
    for cp in m_z:
        cp.wait_recv()
    s_cps = []
    for i, device in enumerate(y_dev + w_dev + [c_dev]):
        cp = remote(segs.at[:, ring], segs.at[:, ring], ms.at[i], mr.at[i], device)
        cp.start()
        s_cps.append(cp)
    items = list(range(3, 3 + 2 * PARTS))
    for p, item in enumerate(items):
        rows_over_z(item)
        if p < 4:
            pass_on(p)
    for p in range(len(items), 4):
        pass_on(p)

    for cp in big_z + c_cps + f_cps + s_cps:
        cp.wait()
    for row in x_cps:
        for cp in row:
            cp.wait_send()
    for cp in m_z + kv_z:
        cp.wait_send()
    for row in y_cps:
        for cp in row:
            cp.wait_send()


def nt(a, b):
    return lax.dot_general(a, b, (((1,), (1,)), ((), ())), preferred_element_type=F32)


def tn(a, b):
    return lax.dot_general(a, b, (((0,), (0,)), ((), ())), preferred_element_type=F32)


def nn(a, b):
    return lax.dot_general(a, b, (((1,), (0,)), ((), ())), preferred_element_type=F32)


def attend_kernel(q, g, kv, segs, att, dq, dkv, qs, gs, scores, acc, total):
    step = pl.program_id(0)
    ring = lax.rem(lax.axis_index("ctx"), 8)
    block = step * RING + ring
    scale = 1.0 / math.sqrt(HEAD)
    log2e = scale / math.log(2.0)

    @pl.when(step == 0)
    def _():
        total[...] = jnp.zeros_like(total)

    for h in range(GROUP):
        qs[h * BLK : (h + 1) * BLK, :] = q[0, :, h * HEAD : (h + 1) * HEAD]
        gs[h * BLK : (h + 1) * BLK, :] = g[0, :, h * HEAD : (h + 1) * HEAD]

    ids = segs[:, 0, :]
    counts = jnp.concatenate(
        [jnp.sum(jnp.where(ids < t, 1.0, 0.0), axis=0, keepdims=True) for t in range(DOCS)], axis=0
    )
    starts = jnp.sum(counts, axis=1, keepdims=True)
    mine = segs[block, 0:1, :]
    doc = lax.broadcasted_iota(jnp.int32, (DOCS, BLK), 0)
    first = jnp.sum(jnp.where(doc == mine, starts, 0.0), axis=0, keepdims=True)
    lowest = jnp.min(first).astype(jnp.int32)
    first = first.astype(jnp.int32)
    here = block * BLK + lax.broadcasted_iota(jnp.int32, (1, BLK), 1)
    begin = lax.div(lowest, CHUNK)
    end = lax.div(block, CHUNK // BLK) + 1

    def keys_of(j):
        return pl.ds(pl.multiple_of(j * CHUNK, CHUNK), CHUNK)

    def score_step(j, top):
        s = nt(kv[keys_of(j), 0:HEAD], qs[...])
        pos = j * CHUNK + lax.broadcasted_iota(jnp.int32, (CHUNK, BLK), 0)
        seen = (pos >= first) & (pos <= here)
        tops = []
        for h in range(GROUP):
            sl = slice(h * BLK, (h + 1) * BLK)
            sh = jnp.where(seen, s[:, sl], NEG)
            scores[j - begin, :, sl] = sh
            tops.append(jnp.max(sh, axis=0, keepdims=True))
        return jnp.maximum(top, jnp.concatenate(tops, axis=1))

    top = lax.fori_loop(begin, end, score_step, jnp.full((1, GW), NEG, F32))
    acc[...] = jnp.zeros_like(acc)

    def out_step(j, norm):
        p = jnp.exp2((scores[j - begin] - top) * log2e)
        scores[j - begin] = p
        acc[...] += tn(kv[keys_of(j), HEAD : 2 * HEAD], p.astype(BF16))
        return norm + jnp.sum(p, axis=0, keepdims=True)

    norm = lax.fori_loop(begin, end, out_step, jnp.zeros((1, GW), F32))
    inv = 1.0 / norm
    deltas = []
    for h in range(GROUP):
        sl = slice(h * BLK, (h + 1) * BLK)
        o = jnp.transpose(acc[:, sl] * inv[:, sl]).astype(BF16)
        att[0, :, sl] = o
        prod = gs[sl, :].astype(F32) * o.astype(F32)
        deltas.append(jnp.sum(jnp.transpose(prod), axis=0, keepdims=True))
    delta = jnp.concatenate(deltas, axis=1)
    acc[...] = jnp.zeros_like(acc)

    def grad_step(j, carry):
        rows = keys_of(j)
        w = scores[j - begin] * inv
        dp = nt(kv[rows, HEAD : 2 * HEAD], gs[...])
        ds = (w * (dp - delta)).astype(BF16)
        acc[...] += tn(kv[rows, 0:HEAD], ds)
        total[rows, 0:HEAD] += nn(ds, qs[...])
        total[rows, HEAD : 2 * HEAD] += nn(w.astype(BF16), gs[...])
        return carry

    lax.fori_loop(begin, end, grad_step, 0)
    for h in range(GROUP):
        sl = slice(h * BLK, (h + 1) * BLK)
        dq[0, :, sl] = jnp.transpose(acc[:, sl] * scale).astype(BF16)

    @pl.when(step == SIDE - 1)
    def _():
        dkv[:, 0:HEAD] = (total[:, 0:HEAD] * scale).astype(BF16)
        dkv[:, HEAD : 2 * HEAD] = total[:, HEAD : 2 * HEAD].astype(BF16)


def return_kernel(
    att, dq, dkv, planes,
    o_att, o_dq, o_k, o_v,
    r_a, r_d, r_kv, c_in, tot, y_in, fin, s_a, s_d, s_kv,
    xs, xr, zs, zr, ys, yr, cs, cr,
):
    x, z, y, core = place()
    x_dev = [(ahead(x, o), ctx_of(z, y, core)) for o in OFFSETS]
    z_dev = [(x, ctx_of(ahead(z, o), y, core)) for o in OFFSETS]
    y_dev = [(x, ctx_of(z, ahead(y, o), core)) for o in OFFSETS]
    c_dev = (x, ctx_of(z, y, 1 - core))
    enter(x_dev + z_dev + y_dev + [c_dev])

    owners = [ahead(y, o) for o in OFFSETS] + [y]
    c_cps = []
    for i, owner in enumerate(owners):
        cp = remote(dkv.at[:, owner, 1 - core], c_in.at[i], cs.at[i], cr.at[i], c_dev)
        cp.start()
        c_cps.append(cp)
    z_cps = []
    for item in range(2 * PARTS):
        src, land = ((att, r_a), (dq, r_d))[item // PARTS]
        rows = pl.ds((item % PARTS) * PART, PART)
        row = []
        for i, o in enumerate(OFFSETS):
            cp = remote(src.at[ahead(z, o), rows], land.at[z, rows], zs.at[i, item], zr.at[i, item], z_dev[i])
            cp.start()
            row.append(cp)
        z_cps.append(row)
    r_a[z] = att[z]
    r_d[z] = dq[z]
    y_cps = []
    for i, owner in enumerate(owners):
        c_cps[i].wait_recv()
        for b in range(SIDE):
            tot[i, b] = (dkv[b, owner, core].astype(F32) + c_in[i, b].astype(F32)).astype(BF16)
        if i < 3:
            cp = remote(tot.at[i], y_in.at[i], ys.at[i], yr.at[i], y_dev[i])
            cp.start()
            y_cps.append(cp)

    x_cps = []
    hots = [[one_hot(planes[ahead(x, o), 1:2, :], s) for s in range(SIDE)] for o in OFFSETS]
    own_hot = [one_hot(planes[x, 1:2, :], s) for s in range(SIDE)]

    def rows_over_x(item):
        which, part = item // PARTS, item % PARTS
        land, stage, out = ((r_a, s_a, o_att), (r_d, s_d, o_dq))[which]
        rows = pl.ds(part * PART, PART)
        for cp in z_cps[item]:
            cp.wait_recv()
        got = [land[s, part * PART : (part + 1) * PART] for s in range(SIDE)]
        for i in range(3):
            put(stage.at[i, rows], pick(hots[i], got))
            cp = remote(
                stage.at[i, rows], out.at[rows, lanes(x, GW)], xs.at[i, item], xr.at[i, item], x_dev[i]
            )
            cp.start()
            x_cps.append(cp)
        put(out.at[rows], pick(own_hot, got), x * GW)

    for item in range(2 * PARTS - 1):
        rows_over_x(item)

    for cp in y_cps:
        cp.wait_recv()
    f_cps = []
    for i, o in enumerate(OFFSETS):
        b = ahead(z, o)
        total = tot[3, b].astype(F32)
        for n in range(3):
            total = total + y_in[n, b].astype(F32)
        fin[i] = total.astype(BF16)
        cp = remote(fin.at[i], r_kv.at[z], zs.at[i, 2 * PARTS], zr.at[i, 2 * PARTS], z_dev[i])
        cp.start()
        f_cps.append(cp)
    total = tot[3, z].astype(F32)
    for n in range(3):
        total = total + y_in[n, z].astype(F32)
    r_kv[z] = total.astype(BF16)

    rows_over_x(2 * PARTS - 1)
    for cp in f_cps:
        cp.wait_recv()
    got = [r_kv[s] for s in range(SIDE)]
    for i in range(3):
        put(s_kv.at[i], pick(hots[i], got))
        for n, out in enumerate((o_k, o_v)):
            item = 2 * PARTS + n
            cp = remote(
                s_kv.at[i, :, pl.ds(n * HEAD, HEAD)], out.at[:, lanes(x, HEAD)],
                xs.at[i, item], xr.at[i, item], x_dev[i],
            )
            cp.start()
            x_cps.append(cp)
    mine = pick(own_hot, got)
    o_k[:, lanes(x, HEAD)] = mine[0]
    o_v[:, lanes(x, HEAD)] = mine[1]

    for cp in x_cps:
        cp.wait()
    for cp in c_cps + y_cps + f_cps:
        cp.wait_send()
    for row in z_cps:
        for cp in row:
            cp.wait_send()


def body(queries, key_rows, value_rows, out_grad, segment_ids, block_plan):
    vmem = pl.BlockSpec(memory_space=pltpu.VMEM)
    dma = pltpu.SemaphoreType.DMA
    shape = jax.ShapeDtypeStruct
    qb, gb, kv, segs, planes = pl.pallas_call(
        gather_kernel,
        out_shape=(
            shape((SIDE, BLK, GW), BF16),
            shape((SIDE, BLK, GW), BF16),
            shape((SIDE, RING, BLK, 2 * HEAD), BF16),
            shape((SIDE, RING, 8, 128), jnp.int32),
            shape((SIDE, 8, 128), jnp.int32),
        ),
        in_specs=[vmem] * 6,
        out_specs=(vmem,) * 5,
        scratch_shapes=[
            pltpu.VMEM((8, 128), jnp.int32),
            pltpu.VMEM((SIDE, BLK, 2 * HEAD), BF16),
            pltpu.VMEM((SIDE, BLK, GW), BF16),
            pltpu.VMEM((SIDE, BLK, GW), BF16),
            pltpu.VMEM((3, BLK, 2 * HEAD), BF16),
            pltpu.VMEM((3, BLK, GW), BF16),
            pltpu.VMEM((3, BLK, GW), BF16),
            dma((3, 3 + 2 * PARTS)),
            dma((3, 3 + 2 * PARTS)),
            dma((3, 2 + 2 * PARTS)),
            dma((3, 2 + 2 * PARTS)),
            dma((4, 3)),
            dma((4, 3)),
            dma((4,)),
            dma((4,)),
            dma((4, 3)),
            dma((4, 3)),
            dma((7,)),
            dma((7,)),
        ],
        compiler_params=pltpu.CompilerParams(
            collective_id=0, has_side_effects=True, vmem_limit_bytes=40 << 20
        ),
        name="gather_rows",
    )(queries[0], key_rows[0], value_rows[0], out_grad[0], segment_ids, block_plan)

    rows = pl.BlockSpec((1, BLK, GW), lambda i: (i, 0, 0))
    length = NBLK * BLK
    att, dq, dkv = pl.pallas_call(
        attend_kernel,
        grid=(SIDE,),
        out_shape=(
            shape((SIDE, BLK, GW), BF16),
            shape((SIDE, BLK, GW), BF16),
            shape((length, 2 * HEAD), BF16),
        ),
        in_specs=[
            rows,
            rows,
            pl.BlockSpec((length, 2 * HEAD), lambda i: (0, 0)),
            pl.BlockSpec((NBLK, 8, 128), lambda i: (0, 0, 0)),
        ],
        out_specs=(rows, rows, pl.BlockSpec((length, 2 * HEAD), lambda i: (0, 0))),
        scratch_shapes=[
            pltpu.VMEM((GROUP * BLK, HEAD), BF16),
            pltpu.VMEM((GROUP * BLK, HEAD), BF16),
            pltpu.VMEM((MOST, CHUNK, GW), F32),
            pltpu.VMEM((HEAD, GW), F32),
            pltpu.VMEM((length, 2 * HEAD), F32),
        ],
        compiler_params=pltpu.CompilerParams(vmem_limit_bytes=48 << 20),
        name="attend",
    )(qb, gb, kv.reshape(length, 2 * HEAD), segs.reshape(NBLK, 8, 128))

    o_att, o_dq, o_k, o_v = pl.pallas_call(
        return_kernel,
        out_shape=(
            shape((BLK, SIDE * GW), BF16),
            shape((BLK, SIDE * GW), BF16),
            shape((BLK, SIDE * HEAD), BF16),
            shape((BLK, SIDE * HEAD), BF16),
        ),
        in_specs=[vmem] * 4,
        out_specs=(vmem,) * 4,
        scratch_shapes=[
            pltpu.VMEM((SIDE, BLK, GW), BF16),
            pltpu.VMEM((SIDE, BLK, GW), BF16),
            pltpu.VMEM((SIDE, BLK, 2 * HEAD), BF16),
            pltpu.VMEM((SIDE, SIDE, BLK, 2 * HEAD), BF16),
            pltpu.VMEM((SIDE, SIDE, BLK, 2 * HEAD), BF16),
            pltpu.VMEM((3, SIDE, BLK, 2 * HEAD), BF16),
            pltpu.VMEM((3, BLK, 2 * HEAD), BF16),
            pltpu.VMEM((3, BLK, GW), BF16),
            pltpu.VMEM((3, BLK, GW), BF16),
            pltpu.VMEM((3, BLK, 2 * HEAD), BF16),
            dma((3, 2 + 2 * PARTS)),
            dma((3, 2 + 2 * PARTS)),
            dma((3, 1 + 2 * PARTS)),
            dma((3, 1 + 2 * PARTS)),
            dma((3,)),
            dma((3,)),
            dma((4,)),
            dma((4,)),
        ],
        compiler_params=pltpu.CompilerParams(
            collective_id=1, has_side_effects=True, vmem_limit_bytes=40 << 20
        ),
        name="return_rows",
    )(att, dq, dkv.reshape(SIDE, SIDE, 2, BLK, 2 * HEAD), planes)
    return o_att[None], o_dq[None], o_k[None], o_v[None]


def solution(mesh):
    rows = P("dp", "ctx", None)
    return jax.shard_map(
        body,
        mesh=mesh,
        in_specs=(rows, rows, rows, rows, P("dp", "ctx"), P("dp", "ctx")),
        out_specs=(rows,) * 4,
        check_vma=False,
    )
```

time: 616 us -> 95.6 us (0.16)
  waiting for transfers between devices: 255 us -> 0 us
  matrix products: 130 us -> 0 us
  Pallas kernels: 0 us -> 85.2 us
  local copies, waits for them, and re-layouts: 75.2 us -> 8.77 us
  blocking collectives: 63.2 us -> 0 us
  other arithmetic: 57.4 us -> 0 us
  loops' own time: 17.3 us -> 0 us
  between operations: 14.9 us -> 1.33 us
    all_gather x6 -> x0, waiting for transfers between devices: 144 us -> none  [the longest x1 51.5 us: body(): lax.all_gather(kv_local, 'ctx', axis=0, tiled=True)]
    dot_general x56 -> x0, matrix products: 130 us -> none  [the longest x16 43.7 us: masked_scores(): jnp.einsum('tkgd,skd->kgts', query_resident, keys_part, preferred_element...]
    reduce_scatter x1 -> x0, waiting for transfers between devices: 110 us -> none  [body(): lax.psum_scatter(stacked.reshape(packed_length, 2 * key_value_width), 'ct...]
    pallas_call x0 -> x3, Pallas kernels: none -> 85.2 us  [the longest x1 38.2 us: body(): pl.pallas_call(return_kernel, out_shape=(shape((BLK, SIDE * GW), BF16), s...]
    all_gather x3 -> x0, blocking collectives: 55.5 us -> none  [the longest x1 28.7 us: body(): lax.all_gather(own_segs, 'ctx', axis=0, tiled=True)]
    reduce_sum x13 -> x0, other arithmetic: 35.4 us -> none  [the longest x8 24.5 us: stat_step(): jnp.sum(jnp.exp(masked - newtop[..., None]), axis=-1)]
    dynamic_update_slice x16 -> x0, local copies, waits for them, and re-layouts: 27.1 us -> none  [body(): query_acc, stacked = lax.scan(grad_step, zero_rows, block_ids)]
    slice x3 -> x0, local copies, waits for them, and re-layouts: 18.6 us -> none  [the longest x2 12.2 us: body(): gathered_key_value[:, key_value_width:]]
  transfers between devices with their start and end apart: 7 -> 0, of which waited for: 6 -> 0; matrix products, arithmetic and copies ran while one was open for 3% -> 0% of each run, Pallas kernels for 0% -> 0%
where the time goes in v1:
time: 95.6 us; the launch traced here: 95.3 us
  Pallas kernels  85.2 us (89%)
  local copies, waits for them, and re-layouts  8.77 us (9%)
  between operations  1.33 us (1%)
    pallas_call x1, Pallas kernels, body(): pl.pallas_call(return_kernel, out_shape=(shape((BLK, SIDE * GW), BF16), s...  38.2 us
    pallas_call x1, Pallas kernels, body(): pl.pallas_call(gather_kernel, out_shape=(shape((SIDE, BLK, GW), BF16), sh...  31 us
    pallas_call x1, Pallas kernels, body(): pl.pallas_call(attend_kernel, grid=(SIDE,), out_shape=(shape((SIDE, BLK,...  15.9 us
    unnamed x16, local copies, waits for them, and re-layouts  8.77 us

profile of v1, /device:TPU:1, one launch (start us, length us, event | category | flops | bytes accessed | tf_op | source)
XLA Modules:
  0.0 95.3 jit_solution(15923317583686988110)
XLA Ops:
  1.3 0.0 copy-start.1
  1.3 1.0 %copy-done.1 = bf16[1,128,2048]{2,1,0:T(8,128)(2,1)S(1)} copy-done((bf16[1,128,2048]{2,1,0:T(8,128)(2,1)S(1)}, bf16[1,128,2048]{2,1,0:T(8,128)(2,1)}, u32[]{:S(2)}) %copy-start.1) | copy-done | bytes 524312
  2.3 0.0 copy-start.2
  2.3 1.0 %copy-done.2 = bf16[1,128,2048]{2,1,0:T(8,128)(2,1)S(1)} copy-done((bf16[1,128,2048]{2,1,0:T(8,128)(2,1)S(1)}, bf16[1,128,2048]{2,1,0:T(8,128)(2,1)}, u32[]{:S(2)}) %copy-start.2) | copy-done | bytes 524312
  3.4 0.0 copy-start.3
  3.4 0.9 copy-done.3
  4.3 0.0 copy-start.4
  4.3 0.9 copy-done.4
  5.2 0.0 copy-start.5
  5.2 0.7 copy-done.5
  5.8 31.0 %gather_rows.1 = (bf16[4,128,512]{2,1,0:T(8,128)(2,1)S(1)}, bf16[4,128,512]{2,1,0:T(8,128)(2,1)S(1)}, bf16[4,8,128,256]{3,2,1,0:T(8,128)(2,1)S(1)}, s32[4,8,8,128]{3,2,1,0:T(8,128)S(1)}, s32[4,8,128]{2,1,0:T(8,128)S(1)}) custom-call(bf16[128,2048]{1,0:T(8,128)(2,1)S(1)} %bitcast.13, bf16[128,512]{1,0:T(8,128)(2,1)S(1)} %bitcast.17, ...), custom_call_target="tpu_custom_call" | custom-call | tf_op jit(solution)/shard_map/gather_rows/pallas_call | solution.py:437
  36.9 0.0 copy-start
  36.9 1.3 %copy-done = bf16[4,8,128,256]{3,2,1,0:T(8,128)(2,1)} copy-done((bf16[4,8,128,256]{3,2,1,0:T(8,128)(2,1)}, bf16[4,8,128,256]{3,2,1,0:T(8,128)(2,1)S(1)}, u32[]{:S(2)}) %copy-start) | copy-done | bytes 2097176
  38.2 15.9 %attend.1 = (bf16[4,128,512]{2,1,0:T(8,128)(2,1)S(1)}, bf16[4,128,512]{2,1,0:T(8,128)(2,1)S(1)}, bf16[4096,256]{1,0:T(8,128)(2,1)S(1)}) custom-call(bf16[4,128,512]{2,1,0:T(8,128)(2,1)S(1)} %get-tuple-element.16.q, bf16[4,128,512]{2,1,0:T(8,128)(2,1)S(1)} %get-tuple-element.17.g, bf16[4096,256]{1,0:T(8,128)(2,1)} %bitcast.12, s32[32,8,128]{2,1,0:T(8,128)S(1)} %bitcast.19), custom_call_target="tpu_custom_call" | custom-call | tf_op jit(solution)/shard_map/attend/pallas_call | solution.py:477
  54.2 38.2 %return_rows.1 = (bf16[128,2048]{1,0:T(8,128)(2,1)S(1)}, bf16[128,2048]{1,0:T(8,128)(2,1)S(1)}, bf16[128,512]{1,0:T(8,128)(2,1)S(1)}, bf16[128,512]{1,0:T(8,128)(2,1)S(1)}) custom-call(bf16[4,128,512]{2,1,0:T(8,128)(2,1)S(1)} %get-tuple-element.20.att, bf16[4,128,512]{2,1,0:T(8,128)(2,1)S(1)} %get-tuple-element.21.dq, ...), custom_call_target="tpu_custom_call" | custom-call | tf_op jit(solution)/shard_map/return_rows/pallas_call | solution.py:503
  92.4 0.8 copy.15
  93.2 0.8 copy.16
  94.0 0.7 copy.17
  94.6 0.7 copy.18
Async XLA Ops:
  1.3 1.0 %copy-start.1 = (bf16[1,128,2048]{2,1,0:T(8,128)(2,1)S(1)}, bf16[1,128,2048]{2,1,0:T(8,128)(2,1)}, u32[]{:S(2)}) copy-start(bf16[1,128,2048]{2,1,0:T(8,128)(2,1)} %param.6) | copy-start | bytes 1572868
  2.3 1.0 %copy-start.2 = (bf16[1,128,2048]{2,1,0:T(8,128)(2,1)S(1)}, bf16[1,128,2048]{2,1,0:T(8,128)(2,1)}, u32[]{:S(2)}) copy-start(bf16[1,128,2048]{2,1,0:T(8,128)(2,1)} %param.9) | copy-start | bytes 1572868
  3.4 0.9 copy-start.3
  4.3 0.9 copy-start.4
  5.2 0.7 copy-start.5
  36.9 1.3 %copy-start = (bf16[4,8,128,256]{3,2,1,0:T(8,128)(2,1)}, bf16[4,8,128,256]{3,2,1,0:T(8,128)(2,1)S(1)}, u32[]{:S(2)}) copy-start(bf16[4,8,128,256]{3,2,1,0:T(8,128)(2,1)S(1)} %get-tuple-element.18) | copy-start | bytes 6291460

commit v2 on v1

--- a/solution.py
+++ b/solution.py
@@ -20,10 +20,11 @@
 NBLK = 32
 DOCS = 16
 OFFSETS = (1, 3, 2)
-CHUNK = 256
-MOST = 10
+CHUNK = 512
+MOST = 5
 PARTS = 2
 PART = BLK // PARTS
+FLIGHT = 2
 NEG = -1e30
 
 
@@ -90,7 +91,7 @@
     q, k, v, g, seg, plan,
     qb, gb, kv, segs, planes,
     meta, a_kv, a_q, a_g, s_kv, s_q, s_g,
-    xs, xr, zs, zr, ys, yr, cs, cr, fs, fr, ms, mr,
+    xs, xr, zs, zr, ys, yr, cs, cr, fs, fr, ms, mr, os,
 ):
     x, z, y, core = place()
     ring = y * 2 + core
@@ -105,7 +106,8 @@
     enter(x_dev + z_dev + y_dev + w_dev + [c_dev])
 
     x_cps = []
-    for item in range(3 + 2 * PARTS):
+
+    def start_x(item):
         row = []
         for i, o in enumerate(OFFSETS):
             t = ahead(x, o)
@@ -123,11 +125,24 @@
             cp.start()
             row.append(cp)
         x_cps.append(row)
+
+    last_item = 2 + 2 * PARTS
+    for item in range(3 + FLIGHT):
+        start_x(item)
     planes[x] = meta[...]
-    a_kv[x, :, 0:HEAD] = k[:, lanes(x, HEAD)]
-    a_kv[x, :, HEAD : 2 * HEAD] = v[:, lanes(x, HEAD)]
-    a_q[x] = q[:, lanes(x, GW)]
-    a_g[x] = g[:, lanes(x, GW)]
+    own = [
+        pltpu.make_async_copy(src, dst, os.at[n])
+        for n, (src, dst) in enumerate(
+            (
+                (k.at[:, lanes(x, HEAD)], a_kv.at[x, :, pl.ds(0, HEAD)]),
+                (v.at[:, lanes(x, HEAD)], a_kv.at[x, :, pl.ds(HEAD, HEAD)]),
+                (q.at[:, lanes(x, GW)], a_q.at[x]),
+                (g.at[:, lanes(x, GW)], a_g.at[x]),
+            )
+        )
+    ]
+    for cp in own:
+        cp.start()
 
     def arrived(item):
         for cp in x_cps[item]:
@@ -144,6 +159,8 @@
     hots = [[one_hot(h, ahead(z, o)) for h in held] for o in OFFSETS]
     own_hot = [one_hot(h, z) for h in held]
 
+    for cp in own:
+        cp.wait()
     arrived(1)
     arrived(2)
     kv_z = []
@@ -185,6 +202,8 @@
         land, stage, out = ((a_q, s_q, qb), (a_g, s_g, gb))[which]
         rows = pl.ds(part * PART, PART)
         arrived(item)
+        if item + FLIGHT <= last_item:
+            start_x(item + FLIGHT)
         got = [land[d, part * PART : (part + 1) * PART] for d in range(SIDE)]
         for i, o in enumerate(OFFSETS):
             put(stage.at[i, rows], pick(hots[i], got))
@@ -205,12 +224,11 @@
         cp.start()
         s_cps.append(cp)
     items = list(range(3, 3 + 2 * PARTS))
-    for p, item in enumerate(items):
+    for n, item in enumerate(items):
         rows_over_z(item)
-        if p < 4:
+        p = n - len(items) + 4
+        if p >= 0:
             pass_on(p)
-    for p in range(len(items), 4):
-        pass_on(p)
 
     for cp in big_z + c_cps + f_cps + s_cps:
         cp.wait()
@@ -236,64 +254,67 @@
     return lax.dot_general(a, b, (((1,), (0,)), ((), ())), preferred_element_type=F32)
 
 
-def attend_kernel(q, g, kv, segs, att, dq, dkv, qs, gs, scores, acc, total):
+def attend_kernel(q, g, kv, segs, att, dq, dkv, qs, gs, scores, acc, total, firsts):
     step = pl.program_id(0)
     ring = lax.rem(lax.axis_index("ctx"), 8)
     block = step * RING + ring
     scale = 1.0 / math.sqrt(HEAD)
     log2e = scale / math.log(2.0)
+    heads = [slice(h * BLK, (h + 1) * BLK) for h in range(GROUP)]
 
     @pl.when(step == 0)
     def _():
         total[...] = jnp.zeros_like(total)
+        ids = segs[:, 0, :]
+        counts = jnp.concatenate(
+            [jnp.sum(jnp.where(ids < t, 1.0, 0.0), axis=0, keepdims=True) for t in range(DOCS)],
+            axis=0,
+        )
+        starts = jnp.sum(counts, axis=1, keepdims=True)
+        doc = lax.broadcasted_iota(jnp.int32, (DOCS, BLK), 0)
+        for n in range(SIDE):
+            mine = segs[n * RING + ring, 0:1, :]
+            found = jnp.sum(jnp.where(doc == mine, starts, 0.0), axis=0, keepdims=True)
+            firsts[n] = jnp.broadcast_to(found.astype(jnp.int32), (8, BLK))
 
     for h in range(GROUP):
-        qs[h * BLK : (h + 1) * BLK, :] = q[0, :, h * HEAD : (h + 1) * HEAD]
-        gs[h * BLK : (h + 1) * BLK, :] = g[0, :, h * HEAD : (h + 1) * HEAD]
-
-    ids = segs[:, 0, :]
-    counts = jnp.concatenate(
-        [jnp.sum(jnp.where(ids < t, 1.0, 0.0), axis=0, keepdims=True) for t in range(DOCS)], axis=0
-    )
-    starts = jnp.sum(counts, axis=1, keepdims=True)
-    mine = segs[block, 0:1, :]
-    doc = lax.broadcasted_iota(jnp.int32, (DOCS, BLK), 0)
-    first = jnp.sum(jnp.where(doc == mine, starts, 0.0), axis=0, keepdims=True)
-    lowest = jnp.min(first).astype(jnp.int32)
-    first = first.astype(jnp.int32)
+        qs[heads[h], :] = q[0, :, heads[h]]
+        gs[heads[h], :] = g[0, :, heads[h]]
+
+    first = firsts[step, 0:1, :]
     here = block * BLK + lax.broadcasted_iota(jnp.int32, (1, BLK), 1)
-    begin = lax.div(lowest, CHUNK)
-    end = lax.div(block, CHUNK // BLK) + 1
+    stop = (block + 1) * BLK
+    lowest = jnp.min(first.astype(F32)).astype(jnp.int32)
+    count = lax.div(stop - lowest + CHUNK - 1, CHUNK)
+    acc[...] = jnp.zeros_like(acc)
 
     def keys_of(j):
-        return pl.ds(pl.multiple_of(j * CHUNK, CHUNK), CHUNK)
+        return pl.multiple_of(jnp.maximum(stop - (j + 1) * CHUNK, 0), BLK)
 
     def score_step(j, top):
-        s = nt(kv[keys_of(j), 0:HEAD], qs[...])
-        pos = j * CHUNK + lax.broadcasted_iota(jnp.int32, (CHUNK, BLK), 0)
-        seen = (pos >= first) & (pos <= here)
+        base = keys_of(j)
+        s = nt(kv[pl.ds(base, CHUNK), 0:HEAD], qs[...])
+        pos = base + lax.broadcasted_iota(jnp.int32, (CHUNK, BLK), 0)
+        seen = (pos >= first) & (pos <= jnp.minimum(here, stop - j * CHUNK - 1))
         tops = []
-        for h in range(GROUP):
-            sl = slice(h * BLK, (h + 1) * BLK)
+        for sl in heads:
             sh = jnp.where(seen, s[:, sl], NEG)
-            scores[j - begin, :, sl] = sh
+            scores[j, :, sl] = sh
             tops.append(jnp.max(sh, axis=0, keepdims=True))
         return jnp.maximum(top, jnp.concatenate(tops, axis=1))
 
-    top = lax.fori_loop(begin, end, score_step, jnp.full((1, GW), NEG, F32))
-    acc[...] = jnp.zeros_like(acc)
+    top = lax.fori_loop(0, count, score_step, jnp.full((1, GW), NEG, F32))
 
     def out_step(j, norm):
-        p = jnp.exp2((scores[j - begin] - top) * log2e)
-        scores[j - begin] = p
-        acc[...] += tn(kv[keys_of(j), HEAD : 2 * HEAD], p.astype(BF16))
+        p = jnp.exp2((scores[j] - top) * log2e)
+        scores[j] = p
+        acc[...] += tn(kv[pl.ds(keys_of(j), CHUNK), HEAD : 2 * HEAD], p.astype(BF16))
         return norm + jnp.sum(p, axis=0, keepdims=True)
 
-    norm = lax.fori_loop(begin, end, out_step, jnp.zeros((1, GW), F32))
+    norm = lax.fori_loop(0, count, out_step, jnp.zeros((1, GW), F32))
     inv = 1.0 / norm
     deltas = []
-    for h in range(GROUP):
-        sl = slice(h * BLK, (h + 1) * BLK)
+    for sl in heads:
         o = jnp.transpose(acc[:, sl] * inv[:, sl]).astype(BF16)
         att[0, :, sl] = o
         prod = gs[sl, :].astype(F32) * o.astype(F32)
@@ -302,8 +323,8 @@
     acc[...] = jnp.zeros_like(acc)
 
     def grad_step(j, carry):
-        rows = keys_of(j)
-        w = scores[j - begin] * inv
+        rows = pl.ds(keys_of(j), CHUNK)
+        w = scores[j] * inv
         dp = nt(kv[rows, HEAD : 2 * HEAD], gs[...])
         ds = (w * (dp - delta)).astype(BF16)
         acc[...] += tn(kv[rows, 0:HEAD], ds)
@@ -311,9 +332,8 @@
         total[rows, HEAD : 2 * HEAD] += nn(w.astype(BF16), gs[...])
         return carry
 
-    lax.fori_loop(begin, end, grad_step, 0)
-    for h in range(GROUP):
-        sl = slice(h * BLK, (h + 1) * BLK)
+    lax.fori_loop(0, count, grad_step, 0)
+    for sl in heads:
         dq[0, :, sl] = jnp.transpose(acc[:, sl] * scale).astype(BF16)
 
     @pl.when(step == SIDE - 1)
@@ -335,10 +355,11 @@
     c_dev = (x, ctx_of(z, y, 1 - core))
     enter(x_dev + z_dev + y_dev + [c_dev])
 
+    blocks = [ahead(z, o) for o in OFFSETS] + [z]
     owners = [ahead(y, o) for o in OFFSETS] + [y]
     c_cps = []
-    for i, owner in enumerate(owners):
-        cp = remote(dkv.at[:, owner, 1 - core], c_in.at[i], cs.at[i], cr.at[i], c_dev)
+    for n, b in enumerate(blocks):
+        cp = remote(dkv.at[b, :, 1 - core], c_in.at[n], cs.at[n], cr.at[n], c_dev)
         cp.start()
         c_cps.append(cp)
     z_cps = []
@@ -354,14 +375,16 @@
     r_a[z] = att[z]
     r_d[z] = dq[z]
     y_cps = []
-    for i, owner in enumerate(owners):
-        c_cps[i].wait_recv()
-        for b in range(SIDE):
-            tot[i, b] = (dkv[b, owner, core].astype(F32) + c_in[i, b].astype(F32)).astype(BF16)
-        if i < 3:
-            cp = remote(tot.at[i], y_in.at[i], ys.at[i], yr.at[i], y_dev[i])
-            cp.start()
-            y_cps.append(cp)
+    for n, b in enumerate(blocks):
+        c_cps[n].wait_recv()
+        row = []
+        for i, owner in enumerate(owners):
+            tot[n, i] = (dkv[b, owner, core].astype(F32) + c_in[n, owner].astype(F32)).astype(BF16)
+            if i < 3:
+                cp = remote(tot.at[n, i], y_in.at[n, i], ys.at[n, i], yr.at[n, i], y_dev[i])
+                cp.start()
+                row.append(cp)
+        y_cps.append(row)
 
     x_cps = []
     hots = [[one_hot(planes[ahead(x, o), 1:2, :], s) for s in range(SIDE)] for o in OFFSETS]
@@ -383,27 +406,26 @@
             x_cps.append(cp)
         put(out.at[rows], pick(own_hot, got), x * GW)
 
-    for item in range(2 * PARTS - 1):
+    f_cps = []
+
+    def owned(n):
+        total = tot[n, 3].astype(F32)
+        for i in range(3):
+            y_cps[n][i].wait_recv()
+            total = total + y_in[n, i].astype(F32)
+        if n < 3:
+            fin[n] = total.astype(BF16)
+            cp = remote(fin.at[n], r_kv.at[z], zs.at[n, 2 * PARTS], zr.at[n, 2 * PARTS], z_dev[n])
+            cp.start()
+            f_cps.append(cp)
+        else:
+            r_kv[z] = total.astype(BF16)
+
+    for item in range(2 * PARTS):
         rows_over_x(item)
-
-    for cp in y_cps:
-        cp.wait_recv()
-    f_cps = []
-    for i, o in enumerate(OFFSETS):
-        b = ahead(z, o)
-        total = tot[3, b].astype(F32)
-        for n in range(3):
-            total = total + y_in[n, b].astype(F32)
-        fin[i] = total.astype(BF16)
-        cp = remote(fin.at[i], r_kv.at[z], zs.at[i, 2 * PARTS], zr.at[i, 2 * PARTS], z_dev[i])
-        cp.start()
-        f_cps.append(cp)
-    total = tot[3, z].astype(F32)
-    for n in range(3):
-        total = total + y_in[n, z].astype(F32)
-    r_kv[z] = total.astype(BF16)
-
-    rows_over_x(2 * PARTS - 1)
+        n = item - 2 * PARTS + 4
+        if n >= 0:
+            owned(n)
     for cp in f_cps:
         cp.wait_recv()
     got = [r_kv[s] for s in range(SIDE)]
@@ -423,15 +445,21 @@
 
     for cp in x_cps:
         cp.wait()
-    for cp in c_cps + y_cps + f_cps:
+    for cp in c_cps + f_cps:
         cp.wait_send()
-    for row in z_cps:
+    for row in z_cps + y_cps:
         for cp in row:
             cp.wait_send()
 
 
+def place_kernel(*refs):
+    for src, dst in zip(refs[:4], refs[4:]):
+        dst[...] = src[...]
+
+
 def body(queries, key_rows, value_rows, out_grad, segment_ids, block_plan):
     vmem = pl.BlockSpec(memory_space=pltpu.VMEM)
+    hbm = pl.BlockSpec(memory_space=pl.ANY)
     dma = pltpu.SemaphoreType.DMA
     shape = jax.ShapeDtypeStruct
     qb, gb, kv, segs, planes = pl.pallas_call(
@@ -443,7 +471,7 @@
             shape((SIDE, RING, 8, 128), jnp.int32),
             shape((SIDE, 8, 128), jnp.int32),
         ),
-        in_specs=[vmem] * 6,
+        in_specs=[hbm] * 4 + [vmem] * 2,
         out_specs=(vmem,) * 5,
         scratch_shapes=[
             pltpu.VMEM((8, 128), jnp.int32),
@@ -465,9 +493,10 @@
             dma((4, 3)),
             dma((7,)),
             dma((7,)),
+            dma((4,)),
         ],
         compiler_params=pltpu.CompilerParams(
-            collective_id=0, has_side_effects=True, vmem_limit_bytes=40 << 20
+            collective_id=0, has_side_effects=True, vmem_limit_bytes=60 << 20
         ),
         name="gather_rows",
     )(queries[0], key_rows[0], value_rows[0], out_grad[0], segment_ids, block_plan)
@@ -495,8 +524,9 @@
             pltpu.VMEM((MOST, CHUNK, GW), F32),
             pltpu.VMEM((HEAD, GW), F32),
             pltpu.VMEM((length, 2 * HEAD), F32),
+            pltpu.VMEM((SIDE, 8, BLK), jnp.int32),
         ],
-        compiler_params=pltpu.CompilerParams(vmem_limit_bytes=48 << 20),
+        compiler_params=pltpu.CompilerParams(vmem_limit_bytes=60 << 20),
         name="attend",
     )(qb, gb, kv.reshape(length, 2 * HEAD), segs.reshape(NBLK, 8, 128))
 
@@ -516,7 +546,7 @@
             pltpu.VMEM((SIDE, BLK, 2 * HEAD), BF16),
             pltpu.VMEM((SIDE, SIDE, BLK, 2 * HEAD), BF16),
             pltpu.VMEM((SIDE, SIDE, BLK, 2 * HEAD), BF16),
-            pltpu.VMEM((3, SIDE, BLK, 2 * HEAD), BF16),
+            pltpu.VMEM((SIDE, 3, BLK, 2 * HEAD), BF16),
             pltpu.VMEM((3, BLK, 2 * HEAD), BF16),
             pltpu.VMEM((3, BLK, GW), BF16),
             pltpu.VMEM((3, BLK, GW), BF16),
@@ -525,17 +555,26 @@
             dma((3, 2 + 2 * PARTS)),
             dma((3, 1 + 2 * PARTS)),
             dma((3, 1 + 2 * PARTS)),
-            dma((3,)),
-            dma((3,)),
+            dma((4, 3)),
+            dma((4, 3)),
             dma((4,)),
             dma((4,)),
         ],
         compiler_params=pltpu.CompilerParams(
-            collective_id=1, has_side_effects=True, vmem_limit_bytes=40 << 20
+            collective_id=1, has_side_effects=True, vmem_limit_bytes=60 << 20
         ),
         name="return_rows",
     )(att, dq, dkv.reshape(SIDE, SIDE, 2, BLK, 2 * HEAD), planes)
-    return o_att[None], o_dq[None], o_k[None], o_v[None]
+    outs = (o_att, o_dq, o_k, o_v)
+    outs = pl.pallas_call(
+        place_kernel,
+        out_shape=tuple(shape(o.shape, BF16) for o in outs),
+        in_specs=[vmem] * 4,
+        out_specs=(vmem,) * 4,
+        compiler_params=pltpu.CompilerParams(vmem_limit_bytes=60 << 20),
+        name="place",
+    )(*outs)
+    return tuple(o[None] for o in outs)
 
 
 def solution(mesh):

time: 95.6 us -> 87.3 us (0.913)
  local copies, waits for them, and re-layouts: 8.77 us -> 0 us
    pallas_call x1, Pallas kernels: 38.2 us -> 29.1 us  [body(): pl.pallas_call(return_kernel, out_shape=(shape((BLK, SIDE * GW), BF16), s...]
    unnamed x16 -> x0, local copies, waits for them, and re-layouts: 8.77 us -> none
    pallas_call x1, Pallas kernels: 15.9 us -> 20.6 us  [body(): pl.pallas_call(attend_kernel, grid=(SIDE,), out_shape=(shape((SIDE, BLK,...]
    pallas_call x1, Pallas kernels: 31 us -> 33.8 us  [body(): pl.pallas_call(gather_kernel, out_shape=(shape((SIDE, BLK, GW), BF16), sh...]
    pallas_call x0 -> x1, Pallas kernels: none -> 2.34 us  [body(): pl.pallas_call(place_kernel, out_shape=tuple((shape(o.shape, BF16) for o...]
where the time goes in v2:
time: 87.3 us; the launch traced here: 87.1 us
  Pallas kernels  85.8 us (98%)
  between operations  1.3 us (1%)
    pallas_call x1, Pallas kernels, body(): pl.pallas_call(gather_kernel, out_shape=(shape((SIDE, BLK, GW), BF16), sh...  33.8 us
    pallas_call x1, Pallas kernels, body(): pl.pallas_call(return_kernel, out_shape=(shape((BLK, SIDE * GW), BF16), s...  29.1 us
    pallas_call x1, Pallas kernels, body(): pl.pallas_call(attend_kernel, grid=(SIDE,), out_shape=(shape((SIDE, BLK,...  20.6 us
    pallas_call x1, Pallas kernels, body(): pl.pallas_call(place_kernel, out_shape=tuple((shape(o.shape, BF16) for o...  2.34 us

profile of v2, /device:TPU:1, one launch (start us, length us, event | category | flops | bytes accessed | tf_op | source)
XLA Modules:
  0.0 87.1 jit_solution(3719813589832301345)
XLA Ops:
  1.3 33.8 %gather_rows.1 = (bf16[4,128,512]{2,1,0:T(8,128)(2,1)}, bf16[4,128,512]{2,1,0:T(8,128)(2,1)}, bf16[4,8,128,256]{3,2,1,0:T(8,128)(2,1)}, s32[4,8,8,128]{3,2,1,0:T(8,128)}, s32[4,8,128]{2,1,0:T(8,128)}) custom-call(bf16[128,2048]{1,0:T(8,128)(2,1)} %bitcast.13, bf16[128,512]{1,0:T(8,128)(2,1)} %bitcast.15, bf16[128,512]{1,0:T(8,128)(2,1)} %bitcast.16, ...), custom_call_target="tpu_custom_call" | custom-call | tf_op jit(solution)/shard_map/gather_rows/pallas_call | solution.py:465
  35.1 20.6 %attend.1 = (bf16[4,128,512]{2,1,0:T(8,128)(2,1)}, bf16[4,128,512]{2,1,0:T(8,128)(2,1)}, bf16[4096,256]{1,0:T(8,128)(2,1)}) custom-call(bf16[4,128,512]{2,1,0:T(8,128)(2,1)} %get-tuple-element.20.q, bf16[4,128,512]{2,1,0:T(8,128)(2,1)} %get-tuple-element.21.g, bf16[4096,256]{1,0:T(8,128)(2,1)} %bitcast.12, s32[32,8,128]{2,1,0:T(8,128)} %bitcast.17), custom_call_target="tpu_custom_call" | custom-call | tf_op jit(solution)/shard_map/attend/pallas_call | solution.py:506
  55.7 29.1 %return_rows.1 = (bf16[128,2048]{1,0:T(8,128)(2,1)}, bf16[128,2048]{1,0:T(8,128)(2,1)}, bf16[128,512]{1,0:T(8,128)(2,1)}, bf16[128,512]{1,0:T(8,128)(2,1)}) custom-call(bf16[4,128,512]{2,1,0:T(8,128)(2,1)} %get-tuple-element.24.att, bf16[4,128,512]{2,1,0:T(8,128)(2,1)} %get-tuple-element.25.dq, bf16[4,4,2,128,256]{4,3,2,1,0:T(8,128)(2,1)} %bitcast.11, ...), custom_call_target="tpu_custom_call" | custom-call | tf_op jit(solution)/shard_map/return_rows/pallas_call | solution.py:533
  84.7 2.3 %place.1 = (bf16[128,2048]{1,0:T(8,128)(2,1)}, bf16[128,2048]{1,0:T(8,128)(2,1)}, bf16[128,512]{1,0:T(8,128)(2,1)}, bf16[128,512]{1,0:T(8,128)(2,1)}) custom-call(bf16[128,2048]{1,0:T(8,128)(2,1)} %get-tuple-element.28.refs_0_, bf16[128,2048]{1,0:T(8,128)(2,1)} %get-tuple-element.29.refs_1_, bf16[128,512]{1,0:T(8,128)(2,1)} %get-tuple-element.30.refs_2_, ...), custom_call_target="tpu_custom_call" | custom-call | tf_op jit(solution)/shard_map/place/pallas_call | solution.py:569

commit v3 on v2

--- a/solution.py
+++ b/solution.py
@@ -1,3 +1,4 @@
+import functools
 import math
 
 import jax
@@ -20,8 +21,9 @@
 NBLK = 32
 DOCS = 16
 OFFSETS = (1, 3, 2)
-CHUNK = 512
-MOST = 5
+CHUNK = 256
+MOST = 10
+SIZES = (1, 2, 3, 4, 5, 6, 8, 10)
 PARTS = 2
 PART = BLK // PARTS
 FLIGHT = 2
@@ -254,7 +256,7 @@
     return lax.dot_general(a, b, (((1,), (0,)), ((), ())), preferred_element_type=F32)
 
 
-def attend_kernel(q, g, kv, segs, att, dq, dkv, qs, gs, scores, acc, total, firsts):
+def attend_kernel(q, g, kv, segs, att, dq, dkv, qs, gs, scores, acc, total, firsts, halves, grads):
     step = pl.program_id(0)
     ring = lax.rem(lax.axis_index("ctx"), 8)
     block = step * RING + ring
@@ -286,55 +288,68 @@
     stop = (block + 1) * BLK
     lowest = jnp.min(first.astype(F32)).astype(jnp.int32)
     count = lax.div(stop - lowest + CHUNK - 1, CHUNK)
-    acc[...] = jnp.zeros_like(acc)
-
     def keys_of(j):
         return pl.multiple_of(jnp.maximum(stop - (j + 1) * CHUNK, 0), BLK)
 
-    def score_step(j, top):
-        base = keys_of(j)
-        s = nt(kv[pl.ds(base, CHUNK), 0:HEAD], qs[...])
-        pos = base + lax.broadcasted_iota(jnp.int32, (CHUNK, BLK), 0)
-        seen = (pos >= first) & (pos <= jnp.minimum(here, stop - j * CHUNK - 1))
-        tops = []
+    def steps(n):
+        top = jnp.full((1, GW), NEG, F32)
+        for j in range(n):
+            base = keys_of(j)
+            s = nt(kv[pl.ds(base, CHUNK), 0:HEAD], qs[...])
+            pos = base + lax.broadcasted_iota(jnp.int32, (CHUNK, BLK), 0)
+            seen = (pos >= first) & (pos <= jnp.minimum(here, stop - j * CHUNK - 1))
+            tops = []
+            for sl in heads:
+                sh = jnp.where(seen, s[:, sl], NEG)
+                scores[j, :, sl] = sh
+                tops.append(jnp.max(sh, axis=0, keepdims=True))
+            top = jnp.maximum(top, jnp.concatenate(tops, axis=1))
+
+        acc[...] = jnp.zeros_like(acc)
+
+        def add_out(j):
+            acc[...] += tn(kv[pl.ds(keys_of(j), CHUNK), HEAD : 2 * HEAD], halves[j])
+
+        norm = jnp.zeros((1, GW), F32)
+        for j in range(n):
+            if j > 0:
+                add_out(j - 1)
+            p = jnp.exp2((scores[j] - top) * log2e)
+            scores[j] = p
+            halves[j] = p.astype(BF16)
+            norm = norm + jnp.sum(p, axis=0, keepdims=True)
+        add_out(n - 1)
+        inv = 1.0 / norm
+        deltas = []
         for sl in heads:
-            sh = jnp.where(seen, s[:, sl], NEG)
-            scores[j, :, sl] = sh
-            tops.append(jnp.max(sh, axis=0, keepdims=True))
-        return jnp.maximum(top, jnp.concatenate(tops, axis=1))
-
-    top = lax.fori_loop(0, count, score_step, jnp.full((1, GW), NEG, F32))
-
-    def out_step(j, norm):
-        p = jnp.exp2((scores[j] - top) * log2e)
-        scores[j] = p
-        acc[...] += tn(kv[pl.ds(keys_of(j), CHUNK), HEAD : 2 * HEAD], p.astype(BF16))
-        return norm + jnp.sum(p, axis=0, keepdims=True)
-
-    norm = lax.fori_loop(0, count, out_step, jnp.zeros((1, GW), F32))
-    inv = 1.0 / norm
-    deltas = []
-    for sl in heads:
-        o = jnp.transpose(acc[:, sl] * inv[:, sl]).astype(BF16)
-        att[0, :, sl] = o
-        prod = gs[sl, :].astype(F32) * o.astype(F32)
-        deltas.append(jnp.sum(jnp.transpose(prod), axis=0, keepdims=True))
-    delta = jnp.concatenate(deltas, axis=1)
-    acc[...] = jnp.zeros_like(acc)
-
-    def grad_step(j, carry):
-        rows = pl.ds(keys_of(j), CHUNK)
-        w = scores[j] * inv
-        dp = nt(kv[rows, HEAD : 2 * HEAD], gs[...])
-        ds = (w * (dp - delta)).astype(BF16)
-        acc[...] += tn(kv[rows, 0:HEAD], ds)
-        total[rows, 0:HEAD] += nn(ds, qs[...])
-        total[rows, HEAD : 2 * HEAD] += nn(w.astype(BF16), gs[...])
-        return carry
-
-    lax.fori_loop(0, count, grad_step, 0)
-    for sl in heads:
-        dq[0, :, sl] = jnp.transpose(acc[:, sl] * scale).astype(BF16)
+            o = jnp.transpose(acc[:, sl] * inv[:, sl]).astype(BF16)
+            att[0, :, sl] = o
+            prod = gs[sl, :].astype(F32) * o.astype(F32)
+            deltas.append(jnp.sum(jnp.transpose(prod), axis=0, keepdims=True))
+        delta = jnp.concatenate(deltas, axis=1)
+        acc[...] = jnp.zeros_like(acc)
+
+        def add_grads(j):
+            rows = pl.ds(keys_of(j), CHUNK)
+            acc[...] += tn(kv[rows, 0:HEAD], grads[j])
+            total[rows, 0:HEAD] += nn(grads[j], qs[...])
+            total[rows, HEAD : 2 * HEAD] += nn(halves[j], gs[...])
+
+        for j in range(n):
+            dp = nt(kv[pl.ds(keys_of(j), CHUNK), HEAD : 2 * HEAD], gs[...])
+            if j > 0:
+                add_grads(j - 1)
+            w = scores[j] * inv
+            grads[j] = (w * (dp - delta)).astype(BF16)
+            halves[j] = w.astype(BF16)
+        add_grads(n - 1)
+        for sl in heads:
+            dq[0, :, sl] = jnp.transpose(acc[:, sl] * scale).astype(BF16)
+
+    below = 0
+    for n in SIZES:
+        pl.when((count > below) & (count <= n))(functools.partial(steps, n))
+        below = n
 
     @pl.when(step == SIDE - 1)
     def _():
@@ -525,6 +540,8 @@
             pltpu.VMEM((HEAD, GW), F32),
             pltpu.VMEM((length, 2 * HEAD), F32),
             pltpu.VMEM((SIDE, 8, BLK), jnp.int32),
+            pltpu.VMEM((MOST, CHUNK, GW), BF16),
+            pltpu.VMEM((MOST, CHUNK, GW), BF16),
         ],
         compiler_params=pltpu.CompilerParams(vmem_limit_bytes=60 << 20),
         name="attend",

time: 87.3 us -> 83.2 us (0.953)
  Pallas kernels: 85.8 us -> 81.7 us
    pallas_call x1, Pallas kernels: 20.6 us -> 16.9 us  [body(): pl.pallas_call(attend_kernel, grid=(SIDE,), out_shape=(shape((SIDE, BLK,...]
where the time goes in v3:
time: 83.2 us; the launch traced here: 83 us
  Pallas kernels  81.7 us (98%)
  between operations  1.3 us (2%)
    pallas_call x1, Pallas kernels, body(): pl.pallas_call(gather_kernel, out_shape=(shape((SIDE, BLK, GW), BF16), sh...  33.8 us
    pallas_call x1, Pallas kernels, body(): pl.pallas_call(return_kernel, out_shape=(shape((BLK, SIDE * GW), BF16), s...  28.6 us
    pallas_call x1, Pallas kernels, body(): pl.pallas_call(attend_kernel, grid=(SIDE,), out_shape=(shape((SIDE, BLK,...  16.9 us
    pallas_call x1, Pallas kernels, body(): pl.pallas_call(place_kernel, out_shape=tuple((shape(o.shape, BF16) for o...  2.34 us

profile of v3, /device:TPU:1, one launch (start us, length us, event | category | flops | bytes accessed | tf_op | source)
XLA Modules:
  0.0 83.0 jit_solution(14875983165997305013)
XLA Ops:
  1.3 33.8 %gather_rows.1 = (bf16[4,128,512]{2,1,0:T(8,128)(2,1)}, bf16[4,128,512]{2,1,0:T(8,128)(2,1)}, bf16[4,8,128,256]{3,2,1,0:T(8,128)(2,1)}, s32[4,8,8,128]{3,2,1,0:T(8,128)}, s32[4,8,128]{2,1,0:T(8,128)}) custom-call(bf16[128,2048]{1,0:T(8,128)(2,1)} %bitcast.13, bf16[128,512]{1,0:T(8,128)(2,1)} %bitcast.15, bf16[128,512]{1,0:T(8,128)(2,1)} %bitcast.16, ...), custom_call_target="tpu_custom_call" | custom-call | tf_op jit(solution)/shard_map/gather_rows/pallas_call | solution.py:480
  35.1 16.9 %attend.1 = (bf16[4,128,512]{2,1,0:T(8,128)(2,1)}, bf16[4,128,512]{2,1,0:T(8,128)(2,1)}, bf16[4096,256]{1,0:T(8,128)(2,1)}) custom-call(bf16[4,128,512]{2,1,0:T(8,128)(2,1)} %get-tuple-element.20.q, bf16[4,128,512]{2,1,0:T(8,128)(2,1)} %get-tuple-element.21.g, bf16[4096,256]{1,0:T(8,128)(2,1)} %bitcast.12, s32[32,8,128]{2,1,0:T(8,128)} %bitcast.17), custom_call_target="tpu_custom_call" | custom-call | tf_op jit(solution)/shard_map/attend/pallas_call | solution.py:521
  52.0 28.6 %return_rows.1 = (bf16[128,2048]{1,0:T(8,128)(2,1)}, bf16[128,2048]{1,0:T(8,128)(2,1)}, bf16[128,512]{1,0:T(8,128)(2,1)}, bf16[128,512]{1,0:T(8,128)(2,1)}) custom-call(bf16[4,128,512]{2,1,0:T(8,128)(2,1)} %get-tuple-element.24.att, bf16[4,128,512]{2,1,0:T(8,128)(2,1)} %get-tuple-element.25.dq, bf16[4,4,2,128,256]{4,3,2,1,0:T(8,128)(2,1)} %bitcast.11, ...), custom_call_target="tpu_custom_call" | custom-call | tf_op jit(solution)/shard_map/return_rows/pallas_call | solution.py:550
  80.6 2.3 %place.1 = (bf16[128,2048]{1,0:T(8,128)(2,1)}, bf16[128,2048]{1,0:T(8,128)(2,1)}, bf16[128,512]{1,0:T(8,128)(2,1)}, bf16[128,512]{1,0:T(8,128)(2,1)}) custom-call(bf16[128,2048]{1,0:T(8,128)(2,1)} %get-tuple-element.28.refs_0_, bf16[128,2048]{1,0:T(8,128)(2,1)} %get-tuple-element.29.refs_1_, bf16[128,512]{1,0:T(8,128)(2,1)} %get-tuple-element.30.refs_2_, ...), custom_call_target="tpu_custom_call" | custom-call | tf_op jit(solution)/shard_map/place/pallas_call | solution.py:586

commit v4 on v3

--- a/solution.py
+++ b/solution.py
@@ -468,8 +468,16 @@
 
 
 def place_kernel(*refs):
-    for src, dst in zip(refs[:4], refs[4:]):
-        dst[...] = src[...]
+    srcs, dsts, held, sems = refs[:4], refs[4:8], refs[8:12], refs[12]
+    ins = [pltpu.make_async_copy(srcs[n], held[n], sems.at[0, n]) for n in range(4)]
+    outs = [pltpu.make_async_copy(held[n], dsts[n], sems.at[1, n]) for n in range(4)]
+    for cp in ins:
+        cp.start()
+    for n in range(4):
+        ins[n].wait()
+        outs[n].start()
+    for cp in outs:
+        cp.wait()
 
 
 def body(queries, key_rows, value_rows, out_grad, segment_ids, block_plan):
@@ -586,8 +594,9 @@
     outs = pl.pallas_call(
         place_kernel,
         out_shape=tuple(shape(o.shape, BF16) for o in outs),
-        in_specs=[vmem] * 4,
-        out_specs=(vmem,) * 4,
+        in_specs=[hbm] * 4,
+        out_specs=(hbm,) * 4,
+        scratch_shapes=[pltpu.VMEM(o.shape, BF16) for o in outs] + [dma((2, 4))],
         compiler_params=pltpu.CompilerParams(vmem_limit_bytes=60 << 20),
         name="place",
     )(*outs)

time: 83.2 us -> 83.5 us (level)
  no operation moved by 1% of the time
where the time goes in v4:
time: 83.5 us; the launch traced here: 83.4 us
  Pallas kernels  82.1 us (98%)
  between operations  1.3 us (2%)
    pallas_call x1, Pallas kernels, body(): pl.pallas_call(gather_kernel, out_shape=(shape((SIDE, BLK, GW), BF16), sh...  33.8 us
    pallas_call x1, Pallas kernels, body(): pl.pallas_call(return_kernel, out_shape=(shape((BLK, SIDE * GW), BF16), s...  29.3 us
    pallas_call x1, Pallas kernels, body(): pl.pallas_call(attend_kernel, grid=(SIDE,), out_shape=(shape((SIDE, BLK,...  16.9 us
    pallas_call x1, Pallas kernels, body(): pl.pallas_call(place_kernel, out_shape=tuple((shape(o.shape, BF16) for o...  2.16 us

profile of v4, /device:TPU:1, one launch (start us, length us, event | category | flops | bytes accessed | tf_op | source)
XLA Modules:
  0.0 83.4 jit_solution(13458542934995890252)
XLA Ops:
  1.3 33.8 %gather_rows.1 = (bf16[4,128,512]{2,1,0:T(8,128)(2,1)}, bf16[4,128,512]{2,1,0:T(8,128)(2,1)}, bf16[4,8,128,256]{3,2,1,0:T(8,128)(2,1)}, s32[4,8,8,128]{3,2,1,0:T(8,128)}, s32[4,8,128]{2,1,0:T(8,128)}) custom-call(bf16[128,2048]{1,0:T(8,128)(2,1)} %bitcast.13, bf16[128,512]{1,0:T(8,128)(2,1)} %bitcast.15, bf16[128,512]{1,0:T(8,128)(2,1)} %bitcast.16, ...), custom_call_target="tpu_custom_call" | custom-call | tf_op jit(solution)/shard_map/gather_rows/pallas_call | solution.py:488
  35.1 16.9 %attend.1 = (bf16[4,128,512]{2,1,0:T(8,128)(2,1)}, bf16[4,128,512]{2,1,0:T(8,128)(2,1)}, bf16[4096,256]{1,0:T(8,128)(2,1)}) custom-call(bf16[4,128,512]{2,1,0:T(8,128)(2,1)} %get-tuple-element.20.q, bf16[4,128,512]{2,1,0:T(8,128)(2,1)} %get-tuple-element.21.g, bf16[4096,256]{1,0:T(8,128)(2,1)} %bitcast.12, s32[32,8,128]{2,1,0:T(8,128)} %bitcast.17), custom_call_target="tpu_custom_call" | custom-call | tf_op jit(solution)/shard_map/attend/pallas_call | solution.py:529
  52.0 29.3 %return_rows.1 = (bf16[128,2048]{1,0:T(8,128)(2,1)}, bf16[128,2048]{1,0:T(8,128)(2,1)}, bf16[128,512]{1,0:T(8,128)(2,1)}, bf16[128,512]{1,0:T(8,128)(2,1)}) custom-call(bf16[4,128,512]{2,1,0:T(8,128)(2,1)} %get-tuple-element.24.att, bf16[4,128,512]{2,1,0:T(8,128)(2,1)} %get-tuple-element.25.dq, bf16[4,4,2,128,256]{4,3,2,1,0:T(8,128)(2,1)} %bitcast.11, ...), custom_call_target="tpu_custom_call" | custom-call | tf_op jit(solution)/shard_map/return_rows/pallas_call | solution.py:558
  81.3 2.2 %place.1 = (bf16[128,2048]{1,0:T(8,128)(2,1)}, bf16[128,2048]{1,0:T(8,128)(2,1)}, bf16[128,512]{1,0:T(8,128)(2,1)}, bf16[128,512]{1,0:T(8,128)(2,1)}) custom-call(bf16[128,2048]{1,0:T(8,128)(2,1)} %get-tuple-element.28.refs_0_, bf16[128,2048]{1,0:T(8,128)(2,1)} %get-tuple-element.29.refs_1_, bf16[128,512]{1,0:T(8,128)(2,1)} %get-tuple-element.30.refs_2_, ...), custom_call_target="tpu_custom_call" | custom-call | tf_op jit(solution)/shard_map/place/pallas_call | solution.py:594
